TPU v7x, 32 devices: a whole 2x2x4 slice. The times are simulated.
32 devices in a mesh: groups: 2 (over y), ctx: 4 (over z), tp: 2 (over x), dp: 2 (over core).
Axes of the slice: x: 2, y: 2, z: 4, core: 2. Of those that a mesh axis runs over, the one named last changes fastest.
Arguments:
- kv_rows: bfloat16 [32768, 1024], P(('groups', 'ctx', 'dp'), 'tp'), parts along dimension 0, may hold values from -6 to 6
- basis: bfloat16 [1024, 512], P('tp'), may hold values from -0.1875 to 0.1875
- out_weight: bfloat16 [4096, 4096], P('tp'), may hold values from -0.09375 to 0.09375
- queries: bfloat16 [64, 8, 512], P(('groups', 'ctx', 'dp'), 'tp'), parts along dimension 0, may hold values from -80 to 80
- new_kv: bfloat16 [64, 1024], P(('groups', 'ctx', 'dp')), parts along dimension 0, may hold values from -6 to 6
- owner: int32 [64], P('groups'), parts along dimension 0, may hold values from 0 to 7, as said below
- req_start: int32 [16, 32], P(('groups', 'ctx', 'dp')), parts along dimension 0, may hold values from 0 to 2048, as said below
Outputs:
- mixed: bfloat16 [64, 4096], P(('groups', 'ctx', 'dp'), 'tp'), parts along dimension 0
There are 2 independent parts, one for each index of `groups`. A program takes and returns all parts, laid end to end along the dimension named above; an argument that names none is the same for every part. Nothing has to cross between parts.
Inputs may be any that keep to these rules, and one draw needn't show every extreme that they name: Every owner owns exactly 4 requests. `req_start`: along the requests the starts never fall and begin at 0; a request's piece ends where the next begins. One source's pieces of one owner's requests hold at most 768 rows; 1 owners receive exactly 768 rows from every source, the others share the rest nearly evenly.
All inputs are finite; a program needn't handle non-finite values.
Results may differ from a plain program's by a relative error of at most 0.0095.
Values may be sent and summed in bfloat16 or wider, within the bound.
A program may use at most 128 MiB of HBM per device.

v0:
```python
import math

import jax
import jax.numpy as jnp
from jax import lax
from jax.sharding import PartitionSpec as P

HD = 128


def route_rows(owner, req_start, row_count):
    starts = req_start[0]
    req_count = starts.shape[0]
    row_ids = jnp.arange(row_count, dtype=jnp.int32)
    req_ids = jnp.arange(req_count, dtype=jnp.int32)
    inside = (starts[None, :] <= row_ids[:, None]).astype(jnp.int32)
    request_of = jnp.sum(inside, axis=1) - 1
    picked = (request_of[:, None] == req_ids[None, :]).astype(jnp.int32)
    ends = jnp.concatenate([starts[1:], jnp.full((1,), row_count, jnp.int32)])
    pieces = ends - starts
    earlier = ((owner[:, None] == owner[None, :]) & (req_ids[None, :] < req_ids[:, None])).astype(
        jnp.int32
    )
    prior_rows = jnp.sum(earlier * pieces[None, :], axis=1)
    local_rank = jnp.sum(earlier, axis=1)
    target = jnp.sum(picked * owner[None, :], axis=1)
    position = (
        row_ids
        - jnp.sum(picked * starts[None, :], axis=1)
        + jnp.sum(picked * prior_rows[None, :], axis=1)
    )
    slot_tag = jnp.sum(picked * local_rank[None, :], axis=1)
    return (target, position, slot_tag)


def on_device(kv_rows, basis, out_weight, queries, new_kv, owner, req_start):
    owner_count = lax.axis_size("ctx") * lax.axis_size("dp")
    row_count = kv_rows.shape[0]
    slot_cap = 3 * row_count // owner_count
    rank_width = basis.shape[1]
    complete_basis = lax.all_gather(basis, "tp", axis=0, tiled=True)
    feat_width = complete_basis.shape[0]
    target, position, slot_tag = route_rows(owner, req_start, row_count)
    tag_buffer = jnp.full((owner_count, slot_cap), -1, jnp.int32).at[target, position].set(slot_tag)
    partial_value = jnp.dot(kv_rows, basis, preferred_element_type=jnp.float32)
    coeffs = lax.psum(partial_value, "tp").astype(jnp.bfloat16)
    send_buffer = (
        jnp.zeros((owner_count, slot_cap, rank_width), jnp.bfloat16)
        .at[target, position]
        .set(coeffs)
    )
    coefficient_slice = lax.all_to_all(
        send_buffer, ("ctx", "dp"), split_axis=0, concat_axis=0, tiled=True
    )
    tag_part = lax.all_to_all(tag_buffer, ("ctx", "dp"), split_axis=0, concat_axis=0, tiled=True)
    returned_rows = jnp.einsum(
        "kql,bl->kqb", coefficient_slice, complete_basis, preferred_element_type=jnp.float32
    )
    rebuilt = returned_rows.astype(jnp.bfloat16)
    half_width = feat_width // 2
    slot_count = queries.shape[0]
    local_heads = queries.shape[1]
    groups_kv = half_width // HD
    row_total = owner_count * slot_cap
    flat_rows = rebuilt.reshape(row_total, feat_width)
    keys = flat_rows[:, :half_width].reshape(row_total, groups_kv, HD)
    values = flat_rows[:, half_width:].reshape(row_total, groups_kv, HD)
    flat_tags = tag_part.reshape(row_total)
    query_heads = queries.reshape(slot_count, local_heads, groups_kv, HD)
    new_keys = new_kv[:, :half_width].reshape(slot_count, groups_kv, HD)
    new_values = new_kv[:, half_width:].reshape(slot_count, groups_kv, HD)
    scale = 1.0 / math.sqrt(HD)
    scores = (
        jnp.einsum("rjgd,ngd->rjgn", query_heads, keys, preferred_element_type=jnp.float32) * scale
    )
    slot_ids = jnp.arange(slot_count, dtype=jnp.int32)
    live = flat_tags[None, None, None, :] == slot_ids[:, None, None, None]
    scores = jnp.where(live, scores, -1e30)
    own_score = (
        jnp.einsum("rjgd,rgd->rjg", query_heads, new_keys, preferred_element_type=jnp.float32)
        * scale
    )
    top = jnp.maximum(jnp.max(scores, axis=3), own_score)
    weights = jnp.where(live, jnp.exp(scores - top[..., None]), 0.0)
    own_weight = jnp.exp(own_score - top)
    total = jnp.sum(weights, axis=3) + own_weight
    weights = (weights / total[..., None]).astype(jnp.bfloat16)
    own_weight = (own_weight / total).astype(jnp.bfloat16)
    attended = jnp.einsum("rjgn,ngd->rjgd", weights, values, preferred_element_type=jnp.float32)
    attended = (
        attended
        + own_weight.astype(jnp.float32)[..., None] * new_values.astype(jnp.float32)[:, None, :, :]
    )
    attended = attended.astype(jnp.bfloat16).reshape(slot_count, local_heads * half_width)
    out_terms = jnp.dot(attended, out_weight, preferred_element_type=jnp.float32)
    return lax.psum_scatter(out_terms.astype(jnp.bfloat16), "tp", scatter_dimension=1, tiled=True)


def solution(mesh):
    return jax.shard_map(
        on_device,
        mesh=mesh,
        in_specs=(
            P(("groups", "ctx", "dp"), "tp"),
            P("tp", None),
            P("tp", None),
            P(("groups", "ctx", "dp"), "tp", None),
            P(("groups", "ctx", "dp"), None),
            P("groups"),
            P(("groups", "ctx", "dp"), None),
        ),
        out_specs=P(("groups", "ctx", "dp"), "tp"),
        check_vma=False,
    )
```

profile of v0, /device:TPU:0, one launch (start us, length us, event | category | flops | bytes accessed | tf_op | source)
XLA Modules:
  0.0 359.3 jit_solution(1297670422486608855)
XLA Ops:
  6.5 1.6 copy-done
  8.1 4.2 %fusion.27 = f32[2048,512]{1,0:T(8,128)} fusion(bf16[2048,512]{1,0:T(8,128)(2,1)S(1)} %copy-done, bf16[512,512]{1,0:T(8,128)(2,1)} %param.8), kind=kOutput, calls=%fused_computation.59 | convolution fusion | flops 1073741824 | bytes 6815744 | tf_op jit(solution)/shard_map/dot_general | solution.py:45
  12.4 0.6 copy-done.4
  13.5 0.2 select_reduce_fusion
  14.0 8.6 %scatter_custom_fusion.1 = s32[6144]{0:T(1024)} fusion(s32[2048]{0:T(1024)S(1)} %broadcast_select_fusion, s32[2048]{0:T(1024)S(1)} %get-tuple-element.5, s32[]{:T(128)} %constant.12.clone.1), kind=kCustom, calls=%fused_computation.42 | custom fusion | bytes 24580
  22.6 6.3 %all-to-all-start.1 = ((s32[8,1,768]{2,1,0:T(1,128)}), s32[8,1,768]{2,1,0:T(1,128)S(1)}, u32[]{:S(2)}, u32[]{:S(2)}) async-start(s32[8,1,768]{2,1,0:T(1,128)} %bitcast.5), calls=%async_computation.1 | async-start | bytes 49152 | tf_op jit(solution)/shard_map/all_to_all | solution.py:55
  28.9 94.2 %all-reduce.2.cloned.1.call-done = f32[2048,512]{1,0:T(8,128)} async-done(((f32[2048,512]{1,0:T(8,128)}), f32[2048,512]{1,0:T(8,128)}) %all-reduce.2.cloned.1.call-update) | async-done | bytes 4194320 | tf_op jit(solution)/shard_map/psum | solution.py:46
  123.1 13.9 %scatter_custom_fusion = bf16[6144,512]{1,0:T(8,128)(2,1)} fusion(s32[2048]{0:T(1024)S(1)} %broadcast_select_fusion, bf16[]{:T(256)} %constant.10.clone.1, f32[2048,512]{1,0:T(8,128)} %all-reduce.2.cloned.1.call-done), kind=kCustom, calls=%fused_computation.7 | custom fusion | flops 1048576 | bytes 10485762
  137.0 4.9 %all-to-all-start = ((bf16[8,768,512]{2,1,0:T(8,128)(2,1)}), bf16[8,768,512]{2,1,0:T(8,128)(2,1)}, u32[]{:S(2)}, u32[]{:S(2)}) async-start(bf16[8,768,512]{2,1,0:T(8,128)(2,1)} %bitcast.90), calls=%async_computation | async-start | bytes 12582912 | tf_op jit(solution)/shard_map/all_to_all | solution.py:52
  142.0 0.7 all-gather.2.cloned.1.call-update
  142.7 0.2 reduce-scatter.4.cloned.1.call-start
  143.1 23.0 %all-gather.2.cloned.1.call-done = bf16[1024,512]{1,0:T(8,128)(2,1)} async-done(((bf16[512,512]{1,0:T(8,128)(2,1)}), bf16[1024,512]{1,0:T(8,128)(2,1)}) %all-gather.2.cloned.1.call-update) | async-done | bytes 1048592 | tf_op jit(solution)/shard_map/all_gather | solution.py:41
  166.1 114.8 %all-to-all-done = bf16[8,768,512]{2,1,0:T(8,128)(2,1)} async-done(((bf16[8,768,512]{2,1,0:T(8,128)(2,1)}), bf16[8,768,512]{2,1,0:T(8,128)(2,1)}, u32[]{:S(2)}, u32[]{:S(2)}) %all-to-all-start) | async-done | bytes 6291488 | tf_op jit(solution)/shard_map/all_to_all | solution.py:52
  280.9 9.1 %convolution_convert_fusion = bf16[8,768,1024]{2,1,0:T(8,128)(2,1)S(1)} fusion(bf16[8,768,512]{2,1,0:T(8,128)(2,1)} %all-to-all-done, bf16[1024,512]{1,0:T(8,128)(2,1)} %all-gather.2.cloned.1.call-done), kind=kOutput, calls=%fused_computation.5 | convolution fusion | flops 6448742400 | bytes 19922944 | tf_op jit(solution)/shard_map/kql,bl->kqb/dot_general | solution.py:56
  290.0 5.2 %fusion.25 = (bf16[6144,512]{1,0:T(8,128)(2,1)}, bf16[6144,512]{1,0:T(8,128)(2,1)}) fusion(bf16[6144,1024]{1,0:T(8,128)(2,1)S(1)} %bitcast.91), kind=kLoop, calls=%fused_computation.57 | loop fusion | bytes 25165824 | tf_op jit(solution)/shard_map/slice | solution.py:66
  295.2 8.7 %copy.43 = bf16[6144,512]{0,1:T(8,128)(2,1)} copy(bf16[6144,512]{1,0:T(8,128)(2,1)} %get-tuple-element.11) | data formatting | bytes 12582912
  303.9 4.2 %fusion.26 = (f32[4,4,4]{1,0,2:T(4,128)S(1)}, f32[4,4,4,6144]{3,1,0,2:T(4,128)S(1)}) fusion(bf16[6144,4,128,1]{0,2,3,1:T(8,128)(2,1)} %bitcast.93, pred[4,6144]{1,0:T(4,128)(4,1)S(1)} %iota_compare_fusion.2, bf16[4,4,512]{2,1,0:T(4,128)(2,1)S(1)} %copy-done.7), kind=kOutput, calls=%fused_computation.58 | convolution fusion | flops 101842880 | bytes 7905536 | tf_op jit(solution)/shard_map/rjgd,ngd->rjgn/dot_general | solution.py:74
  308.2 0.9 fusion.8
  309.1 8.7 %copy.42 = bf16[6144,512]{0,1:T(8,128)(2,1)} copy(bf16[6144,512]{1,0:T(8,128)(2,1)} %get-tuple-element.12) | data formatting | bytes 12582912
  317.8 5.0 %fusion.6 = bf16[4,4,4,128]{3,1,0,2:T(4,128)(2,1)S(1)} fusion(bf16[6144,4,128,1]{0,2,3,1:T(8,128)(2,1)} %bitcast.92, f32[4,4,4,6144]{3,1,0,2:T(4,128)S(1)} %get-tuple-element.18, f32[4,4,4]{1,0,2:T(4,128)S(1)} %get-tuple-element.14, f32[4,4,4]{1,0,2:T(4,128)S(1)} %bitcast_maximum_fusion, pred[4,6144]{1,0:T(4,128)(4,1)S(1)} %iota_compare_fusion.2, ...), kind=kOutput, calls=%fused_computation.14 | convolution fusion | flops 102260736 | bytes 7914240 | tf_op jit(solution)/shard_map/rjgn,ngd->rjgd/dot_general | solution.py:89
  322.9 8.2 %convolution_convert_fusion.1 = bf16[4,4096]{1,0:T(4,128)(2,1)S(1)} fusion(bf16[4,2048]{1,0:T(4,128)(2,1)S(1)} %reshape.112, bf16[2048,4096]{1,0:T(8,128)(2,1)} %param.9), kind=kOutput, calls=%fused_computation.6 | convolution fusion | flops 67125248 | bytes 16826368 | tf_op jit(solution)/shard_map/dot_general | solution.py:95
  331.1 1.4 copy.40
  332.5 18.4 %reduce-scatter.4.cloned.1.call-done = bf16[2048,4]{1,0:T(8,128)(2,1)} async-done(((bf16[4096,4]{1,0:T(8,128)(2,1)}), bf16[2048,4]{1,0:T(8,128)(2,1)}) %reduce-scatter.4.cloned.1.call-update) | async-done | bytes 16400
  350.9 1.9 copy.41
  (36 shorter events, 1.0 us)
Async XLA Ops:
  6.5 1.6 copy-start
  6.5 116.5 %all-reduce.2.cloned.1.call-start = ((), (), s32[]{:S(2)}) async-start(), calls=%async_computation.3 | async-start | bytes 8388608 | tf_op jit(solution)/shard_map/psum | solution.py:46
  12.3 0.7 copy-start.4
  12.3 0.8 copy-start.3
  12.4 1.4 copy-start.6
  12.4 1.5 copy-start.5
  22.6 114.4 %all-to-all-start.1 = ((s32[8,1,768]{2,1,0:T(1,128)}), s32[8,1,768]{2,1,0:T(1,128)S(1)}, u32[]{:S(2)}, u32[]{:S(2)}) async-start(s32[8,1,768]{2,1,0:T(1,128)} %bitcast.5), calls=%async_computation.1 | async-start | bytes 49152 | tf_op jit(solution)/shard_map/all_to_all | solution.py:55
  137.0 5.9 %copy-start.2 = (bf16[4,1024]{1,0:T(4,128)(2,1)S(1)}, bf16[4,1024]{1,0:T(4,128)(2,1)}, u32[]{:S(2)}) copy-start(bf16[4,1024]{1,0:T(4,128)(2,1)} %param.11) | copy-start | bytes 24580
  137.0 5.9 %copy-start.7 = (bf16[4,4,512]{2,1,0:T(4,128)(2,1)S(1)}, bf16[4,4,512]{2,1,0:T(4,128)(2,1)}, u32[]{:S(2)}) copy-start(bf16[4,4,512]{2,1,0:T(4,128)(2,1)} %param.10) | copy-start | bytes 49156
  137.0 143.8 %all-to-all-start = ((bf16[8,768,512]{2,1,0:T(8,128)(2,1)}), bf16[8,768,512]{2,1,0:T(8,128)(2,1)}, u32[]{:S(2)}, u32[]{:S(2)}) async-start(bf16[8,768,512]{2,1,0:T(8,128)(2,1)} %bitcast.90), calls=%async_computation | async-start | bytes 12582912 | tf_op jit(solution)/shard_map/all_to_all | solution.py:52
  141.9 24.2 %all-gather.2.cloned.1.call-start = ((), (), s32[]{:S(2)}) async-start(), calls=%async_computation.4 | async-start | bytes 1572864 | tf_op jit(solution)/shard_map/all_gather | solution.py:41
  142.7 208.2 %reduce-scatter.4.cloned.1.call-start = ((), (), s32[]{:S(2)}) async-start(), calls=%async_computation.5 | async-start | bytes 1572864
  322.9 29.9 %copy-start.1 = (bf16[2048,512]{1,0:T(8,128)(2,1)S(1)}, bf16[2048,512]{1,0:T(8,128)(2,1)}, u32[]{:S(2)}) copy-start(bf16[2048,512]{1,0:T(8,128)(2,1)} %param.7) | copy-start | bytes 6291460
Sparse Core Ops, SparseCore 0:
  12.5 110.5 all-reduce.1
  144.4 21.6 all-gather.1
  332.6 18.2 reduce-scatter.3
where the time goes:
time: 360 us; the launch traced here: 359 us
  waiting for transfers between devices  251 us (70%)
  local copies, waits for them, and re-layouts  36.8 us (10%)
  matrix products  30.9 us (9%)
  other arithmetic  15.8 us (4%)
  between operations  13.3 us (4%)
  starting transfers between devices  11.5 us (3%)
    all_to_all x1, waiting for transfers between devices, on_device(): lax.all_to_all(send_buffer, ('ctx', 'dp'), split_axis=0, concat_axis=0, t...  115 us
    psum x1, waiting for transfers between devices, on_device(): coeffs = lax.psum(partial_value, 'tp').astype(jnp.bfloat16)  94.2 us
    unnamed x21, local copies, waits for them, and re-layouts  31.6 us
    all_gather x1, waiting for transfers between devices, on_device(): complete_basis = lax.all_gather(basis, 'tp', axis=0, tiled=True)  23 us
    unnamed x4, waiting for transfers between devices  19.1 us
    unnamed x4, other arithmetic  14.1 us
    dot_general x1, matrix products, on_device(): jnp.einsum('kql,bl->kqb', coefficient_slice, complete_basis, preferred_el...  9.15 us
    dot_general x1, matrix products, on_device(): jnp.dot(attended, out_weight, preferred_element_type=jnp.float32)  8.19 us
  transfers between devices with their start and end apart: 5, of which 4 were waited for; matrix products, arithmetic and copies ran while one was open for 7% of the time, Pallas kernels for 0%

commit v1 on v0

v1 whole, which is shorter than its diff:
```python
import math

import jax
import jax.numpy as jnp
from jax import lax
from jax.sharding import PartitionSpec as P

HD = 128


def token_slots(owner, req_start, row_count, slot_own):
    starts = req_start[0]
    req_count = starts.shape[0]
    row_ids = jnp.arange(row_count, dtype=jnp.int32)
    req_ids = jnp.arange(req_count, dtype=jnp.int32)
    inside = (starts[None, :] <= row_ids[:, None]).astype(jnp.int32)
    request_of = jnp.sum(inside, axis=1) - 1
    picked = (request_of[:, None] == req_ids[None, :]).astype(jnp.int32)
    earlier = (owner[:, None] == owner[None, :]) & (req_ids[None, :] < req_ids[:, None])
    slot_of = owner * slot_own + jnp.sum(earlier.astype(jnp.int32), axis=1)
    return jnp.sum(picked * slot_of[None, :], axis=1)


def on_device(kv_rows, basis, out_weight, queries, new_kv, owner, req_start):
    owners = lax.axis_size("ctx") * lax.axis_size("dp")
    rows, feat = kv_rows.shape
    own_slots, local_j, half = queries.shape
    groups = half // HD
    f32, bf16 = jnp.float32, jnp.bfloat16
    scale = 1.0 / math.sqrt(HD)
    whole_basis = lax.all_gather(basis, "tp", axis=0, tiled=True)
    rank = basis.shape[1]
    basis_k = whole_basis[:half].reshape(groups, HD, rank)
    basis_v = whole_basis[half:].reshape(groups, HD, rank)
    q_all = lax.all_gather(queries, ("ctx", "dp"), axis=0, tiled=True)
    q_all = lax.all_gather(q_all, "tp", axis=1, tiled=True)
    slots, heads = q_all.shape[:2]
    q4 = q_all.reshape(slots, heads, groups, HD)
    q_rank = jnp.einsum("rjgd,gdl->grjl", q4, basis_k, preferred_element_type=f32).astype(bf16)
    q_feat = jnp.einsum("grjl,fl->grjf", q_rank, basis, preferred_element_type=f32).astype(bf16)
    slot = token_slots(owner, req_start, rows, own_slots)
    slot_ids = jnp.arange(slots, dtype=jnp.int32)
    live = slot_ids[:, None] == slot[None, :]
    dense = jnp.einsum("grjf,nf->grjn", q_feat, kv_rows, preferred_element_type=f32)
    part = jnp.sum(jnp.where(live[None, :, None, :], dense, 0.0), axis=1)
    score = lax.psum(part, "tp") * scale
    top = jnp.max(jnp.where(live[None, :, None, :], score[:, None], -1e30), axis=3)
    top_tok = jnp.sum(jnp.where(live[None, :, None, :], top[..., None], 0.0), axis=1)
    p = jnp.exp(score - top_tok)
    spread = jnp.where(live[None, :, None, :], p[:, None], 0.0)
    total = jnp.sum(spread, axis=3)
    mixed = jnp.einsum("grjn,nf->grjf", spread.astype(bf16), kv_rows, preferred_element_type=f32)
    mixed = jnp.einsum("grjf,fl->grjl", mixed.astype(bf16), basis, preferred_element_type=f32)
    mixed = jnp.einsum("grjl,gdl->jrgd", mixed.astype(bf16), basis_v, preferred_element_type=f32)
    mixed = lax.psum_scatter(mixed.astype(bf16), "tp", scatter_dimension=0, tiled=True)
    first_j = lax.axis_index("tp") * local_j
    stats = jnp.stack([top, total]).transpose(3, 2, 1, 0)
    stats = lax.dynamic_slice_in_dim(stats, first_j, local_j, axis=0)
    mixed = lax.all_to_all(
        mixed.reshape(local_j, owners, own_slots, groups, HD), ("ctx", "dp"), 1, 1, tiled=True
    ).astype(f32)
    stats = lax.all_to_all(
        stats.reshape(local_j, owners, own_slots, groups, 2), ("ctx", "dp"), 1, 1, tiled=True
    )
    q_own = queries.reshape(own_slots, local_j, groups, HD)
    new_keys = new_kv[:, :half].reshape(own_slots, groups, HD)
    new_values = new_kv[:, half:].reshape(own_slots, groups, HD)
    own = jnp.einsum("rjgd,rgd->jrg", q_own, new_keys, preferred_element_type=f32) * scale
    tops, totals = stats[..., 0], stats[..., 1]
    best = jnp.maximum(jnp.max(tops, axis=1), own)
    lift = jnp.exp(tops - best[:, None])
    own_w = jnp.exp(own - best)
    denom = jnp.sum(lift * totals, axis=1) + own_w
    att = jnp.sum(lift[..., None] * mixed, axis=1)
    att = att + own_w[..., None] * new_values.astype(f32)[None]
    att = (att / denom[..., None]).astype(bf16)
    att = att.transpose(1, 0, 2, 3).reshape(own_slots, local_j * half)
    out = jnp.dot(att, out_weight, preferred_element_type=f32)
    return lax.psum_scatter(out.astype(bf16), "tp", scatter_dimension=1, tiled=True)


def solution(mesh):
    return jax.shard_map(
        on_device,
        mesh=mesh,
        in_specs=(
            P(("groups", "ctx", "dp"), "tp"),
            P("tp", None),
            P("tp", None),
            P(("groups", "ctx", "dp"), "tp", None),
            P(("groups", "ctx", "dp"), None),
            P("groups"),
            P(("groups", "ctx", "dp"), None),
        ),
        out_specs=P(("groups", "ctx", "dp"), "tp"),
        check_vma=False,
    )
```

time: 360 us -> 143 us (0.40)
  waiting for transfers between devices: 251 us -> 54.5 us
  local copies, waits for them, and re-layouts: 36.8 us -> 9.22 us
  blocking collectives: 0 us -> 25.5 us
  matrix products: 30.9 us -> 21.9 us
  other arithmetic: 15.8 us -> 9.44 us
    all_to_all x2, waiting for transfers between devices: 115 us -> 11.1 us  [the longest x1 6.42 us: on_device(): lax.all_to_all(mixed.reshape(local_j, owners, own_slots, groups, HD), ('c...]
    psum x1, waiting for transfers between devices: 94.2 us -> 23.8 us  [on_device(): score = lax.psum(part, 'tp') * scale]
    unnamed x21 -> x12, local copies, waits for them, and re-layouts: 31.6 us -> 4.25 us
    all_gather x0 -> x2, blocking collectives: none -> 25.5 us  [the longest x1 15.9 us: on_device(): q_all = lax.all_gather(queries, ('ctx', 'dp'), axis=0, tiled=True)]
    all_gather x1, waiting for transfers between devices: 23 us -> 0.38 us  [on_device(): whole_basis = lax.all_gather(basis, 'tp', axis=0, tiled=True)]
    unnamed x4 -> x0, other arithmetic: 14.1 us -> none
    dot_general x6, matrix products: 30.9 us -> 21.9 us  [the longest x1 8.04 us: on_device(): out = jnp.dot(att, out_weight, preferred_element_type=f32)]
    slice x2 -> x1, local copies, waits for them, and re-layouts: 5.25 us -> 1.27 us  [on_device(): basis_k = whole_basis[:half].reshape(groups, HD, rank)]
  transfers between devices with their start and end apart: 5 -> 6, of which waited for: 4 -> 5; matrix products, arithmetic and copies ran while one was open for 7% -> 5% of each run, Pallas kernels for 0% -> 0%
where the time goes in v1:
time: 143 us; the launch traced here: 142 us
  waiting for transfers between devices  54.5 us (38%)
  blocking collectives  25.5 us (18%)
  matrix products  21.9 us (15%)
  between operations  13.3 us (9%)
  other arithmetic  9.44 us (7%)
  local copies, waits for them, and re-layouts  9.22 us (6%)
  starting transfers between devices  8.29 us (6%)
    psum x1, waiting for transfers between devices, on_device(): score = lax.psum(part, 'tp') * scale  23.8 us
    unnamed x5, waiting for transfers between devices  19.3 us
    all_gather x1, blocking collectives, on_device(): q_all = lax.all_gather(queries, ('ctx', 'dp'), axis=0, tiled=True)  15.9 us
    all_gather x1, blocking collectives, on_device(): q_all = lax.all_gather(q_all, 'tp', axis=1, tiled=True)  9.61 us
    dot_general x1, matrix products, on_device(): out = jnp.dot(att, out_weight, preferred_element_type=f32)  8.04 us
    all_to_all x1, waiting for transfers between devices, on_device(): lax.all_to_all(mixed.reshape(local_j, owners, own_slots, groups, HD), ('c...  6.42 us
    all_to_all x1, waiting for transfers between devices, on_device(): lax.all_to_all(stats.reshape(local_j, owners, own_slots, groups, 2), ('ct...  4.63 us
    all_to_all x1, starting transfers between devices, on_device(): lax.all_to_all(stats.reshape(local_j, owners, own_slots, groups, 2), ('ct...  4.61 us
  transfers between devices with their start and end apart: 6, of which 5 were waited for; matrix products, arithmetic and copies ran while one was open for 5% of the time, Pallas kernels for 0%

profile of v1, /device:TPU:0, one launch (start us, length us, event | category | flops | bytes accessed | tf_op | source)
XLA Modules:
  0.0 142.1 jit_solution(8865819055171153568)
XLA Ops:
  7.3 0.9 convert_reduce_fusion.1
  9.0 15.9 %all_gather.9 = bf16[32,4,512]{2,1,0:T(4,128)(2,1)S(1)} all-gather(bf16[4,4,512]{2,1,0:T(4,128)(2,1)} %param.10), channel_id=1, replica_groups=mesh['groups'=2,'ctx'=4,'tp'=2,'dp'=2] {'ctx','dp'}, dimensions={0}, use_global_device_ids=true | all-gather | bytes 147456 | tf_op jit(solution)/shard_map/all_gather | solution.py:35
  24.9 9.6 %all_gather.10 = bf16[32,8,512]{2,0,1:T(8,128)(2,1)S(1)} all-gather(bf16[32,4,512]{2,0,1:T(8,128)(2,1)S(1)} %copy.51), channel_id=1, replica_groups=mesh['groups'=2,'ctx'=4,'tp'=2,'dp'=2] {'tp'}, dimensions={1}, use_global_device_ids=true | all-gather | bytes 393216 | tf_op jit(solution)/shard_map/all_gather | solution.py:36
  35.8 1.3 fusion.32
  37.0 3.0 %convolution_convert_fusion.3 = bf16[4,32,8,512]{3,2,1,0:T(8,128)(2,1)} fusion(bf16[4,128,512,1]{2,1,3,0:T(8,128)(2,1)S(1)} %bitcast.112, bf16[512,512]{1,0:T(8,128)(2,1)} %param.8, bf16[32,8,512]{2,0,1:T(8,128)(2,1)S(1)} %all_gather.10), kind=kOutput, calls=%fused_computation.14 | convolution fusion | flops 672137216 | bytes 2359296 | tf_op jit(solution)/shard_map/grjl,fl->grjf/dot_general | solution.py:40
  40.0 4.4 %select_reduce_fusion.3 = f32[4,8,2048]{2,1,0:T(8,128)} fusion(pred[32,2048]{1,0:T(8,128)(4,1)S(1)} %iota_compare_fusion.2, bf16[4,32,8,512]{3,2,1,0:T(8,128)(2,1)} %convolution_convert_fusion.3, bf16[2048,512]{1,0:T(8,128)(2,1)S(1)} %copy-done), kind=kOutput, calls=%fused_computation.4 | convolution fusion | flops 2151612416 | bytes 3473408 | tf_op jit(solution)/shard_map/grjf,nf->grjn/dot_general | solution.py:44
  44.6 23.8 %all-reduce.2.cloned.1.call-done = f32[4,8,2048]{2,1,0:T(8,128)} async-done(((f32[4,8,2048]{2,1,0:T(8,128)}), f32[4,8,2048]{2,1,0:T(8,128)}) %all-reduce.2.cloned.1.call-update) | async-done | bytes 262160 | tf_op jit(solution)/shard_map/psum | solution.py:46
  68.3 1.0 broadcast_multiply_fusion
  69.3 1.1 select_reduce_fusion.2
  70.4 1.0 select_reduce_fusion.1
  71.4 1.0 subtract_exponential_fusion
  72.4 3.3 %fusion.6 = bf16[4,32,8,512]{3,2,1,0:T(8,128)(2,1)} fusion(bf16[2048,512]{1,0:T(8,128)(2,1)S(1)} %copy-done, f32[4,8,2048]{2,1,0:T(8,128)S(1)} %subtract_exponential_fusion, pred[32,2048]{1,0:T(8,128)(4,1)S(1)} %iota_compare_fusion.2), kind=kOutput, calls=%fused_computation.15 | convolution fusion | flops 2150105088 | bytes 3473408 | tf_op jit(solution)/shard_map/grjn,nf->grjf/dot_general | solution.py:52
  75.8 1.7 %select_reduce_fusion = f32[4,32,8]{2,1,0:T(8,128)} fusion(f32[4,8,2048]{2,1,0:T(8,128)S(1)} %subtract_exponential_fusion, pred[32,2048]{1,0:T(8,128)(4,1)S(1)} %iota_compare_fusion.2), kind=kLoop, calls=%fused_computation.1 | loop fusion | flops 4193280 | bytes 331776 | tf_op jit(solution)/shard_map/reduce_sum | solution.py:51
  77.5 2.2 %fusion.11 = bf16[8,32,4,128]{3,0,1,2:T(8,128)(2,1)S(1)} fusion(bf16[4,128,512,1]{2,1,3,0:T(8,128)(2,1)S(1)} %bitcast.111, bf16[4,32,8,512]{3,2,1,0:T(8,128)(2,1)} %fusion.6, bf16[512,512]{1,0:T(8,128)(2,1)S(1)} %copy-done.1), kind=kOutput, calls=%fused_computation.18 | convolution fusion | flops 671744000 | bytes 2359296 | tf_op jit(solution)/shard_map/grjl,gdl->jrgd/dot_general | solution.py:54
  82.0 4.6 %all-to-all-start = ((f32[8,1,128]{2,1,0:T(1,128)}), f32[8,1,128]{2,1,0:T(1,128)S(1)}, u32[]{:S(2)}, u32[]{:S(2)}) async-start(f32[8,1,128]{2,1,0:T(1,128)} %reshape.84), calls=%async_computation | async-start | bytes 8192 | tf_op jit(solution)/shard_map/all_to_all | solution.py:62
  86.6 0.9 fusion.26
  87.5 4.6 %all-to-all-done = f32[8,1,128]{2,1,0:T(1,128)S(1)} async-done(((f32[8,1,128]{2,1,0:T(1,128)}), f32[8,1,128]{2,1,0:T(1,128)S(1)}, u32[]{:S(2)}, u32[]{:S(2)}) %all-to-all-start) | async-done | bytes 4128 | tf_op jit(solution)/shard_map/all_to_all | solution.py:62
  93.6 1.6 %copy.61 = bf16[4,8,4,4,128]{4,0,2,3,1:T(4,128)(2,1)} copy(bf16[4,8,4,4,128]{4,2,1,3,0:T(4,128)(2,1)} %bitcast.114) | data formatting | bytes 262144 | tf_op jit(solution)/shard_map/reshape | solution.py:60
  95.3 3.4 %all-to-all-start.1 = ((bf16[4,8,4,4,128]{4,0,2,3,1:T(4,128)(2,1)}), bf16[4,8,4,4,128]{4,0,2,3,1:T(4,128)(2,1)S(1)}, u32[]{:S(2)}, u32[]{:S(2)}) async-start(bf16[4,8,4,4,128]{4,0,2,3,1:T(4,128)(2,1)} %copy.61), calls=%async_computation.2 | async-start | bytes 262144 | tf_op jit(solution)/shard_map/all_to_all | solution.py:59
  98.9 6.4 %all-to-all-done.1 = bf16[4,8,4,4,128]{4,0,2,3,1:T(4,128)(2,1)S(1)} async-done(((bf16[4,8,4,4,128]{4,0,2,3,1:T(4,128)(2,1)}), bf16[4,8,4,4,128]{4,0,2,3,1:T(4,128)(2,1)S(1)}, u32[]{:S(2)}, u32[]{:S(2)}) %all-to-all-start.1) | async-done | bytes 131104 | tf_op jit(solution)/shard_map/all_to_all | solution.py:59
  105.7 8.0 %convolution_convert_fusion = bf16[4,4096]{1,0:T(4,128)(2,1)S(1)} fusion(bf16[4,2048]{1,0:T(4,128)(2,1)S(1)} %reshape.71, bf16[2048,4096]{1,0:T(8,128)(2,1)} %param.9), kind=kOutput, calls=%fused_computation.5 | convolution fusion | flops 67125248 | bytes 16826368 | tf_op jit(solution)/shard_map/dot_general | solution.py:78
  113.8 1.4 copy.75
  115.2 18.5 %reduce-scatter.7.cloned.1.call-done = bf16[2048,4]{1,0:T(8,128)(2,1)} async-done(((bf16[4096,4]{1,0:T(8,128)(2,1)}), bf16[2048,4]{1,0:T(8,128)(2,1)}) %reduce-scatter.7.cloned.1.call-update) | async-done | bytes 16400
  133.7 1.9 %copy.76 = bf16[4,2048]{1,0:T(4,128)(2,1)} copy(bf16[4,2048]{0,1:T(8,128)(2,1)} %bitcast.109) | data formatting | bytes 32768
  (45 shorter events, 7.2 us)
Async XLA Ops:
  6.5 33.5 %copy-start = (bf16[2048,512]{1,0:T(8,128)(2,1)S(1)}, bf16[2048,512]{1,0:T(8,128)(2,1)}, u32[]{:S(2)}) copy-start(bf16[2048,512]{1,0:T(8,128)(2,1)} %param.7) | copy-start | bytes 6291460
  6.5 29.2 %all-gather.2.cloned.1.call-start = ((), (), s32[]{:S(2)}) async-start(), calls=%async_computation.4 | async-start | bytes 1572864 | tf_op jit(solution)/shard_map/all_gather | solution.py:31
  7.3 61.0 %all-reduce.2.cloned.1.call-start = ((), (), s32[]{:S(2)}) async-start(), calls=%async_computation.5 | async-start | bytes 524288 | tf_op jit(solution)/shard_map/psum | solution.py:46
  40.0 4.5 %copy-start.3 = (bf16[4,1024]{1,0:T(4,128)(2,1)S(1)}, bf16[4,1024]{1,0:T(4,128)(2,1)}, u32[]{:S(2)}) copy-start(bf16[4,1024]{1,0:T(4,128)(2,1)} %param.11) | copy-start | bytes 24580
  44.5 49.1 %reduce-scatter.5.cloned.1.call-start = ((), (), s32[]{:S(2)}) async-start(), calls=%async_computation.6 | async-start | bytes 393216 | tf_op jit(solution)/shard_map/reduce_scatter | solution.py:55
  72.4 5.0 %copy-start.1 = (bf16[512,512]{1,0:T(8,128)(2,1)S(1)}, bf16[512,512]{1,0:T(8,128)(2,1)}, u32[]{:S(2)}) copy-start(bf16[512,512]{1,0:T(8,128)(2,1)} %param.8) | copy-start | bytes 1572868
  77.5 3.1 %copy-start.2 = (f32[4,32,8]{2,1,0:T(8,128)S(1)}, f32[4,32,8]{2,1,0:T(8,128)}, u32[]{:S(2)}) copy-start(f32[4,32,8]{2,1,0:T(8,128)} %select_reduce_fusion) | copy-start | bytes 12292
  82.0 10.1 %all-to-all-start = ((f32[8,1,128]{2,1,0:T(1,128)}), f32[8,1,128]{2,1,0:T(1,128)S(1)}, u32[]{:S(2)}, u32[]{:S(2)}) async-start(f32[8,1,128]{2,1,0:T(1,128)} %reshape.84), calls=%async_computation | async-start | bytes 8192 | tf_op jit(solution)/shard_map/all_to_all | solution.py:62
  95.3 10.1 %all-to-all-start.1 = ((bf16[4,8,4,4,128]{4,0,2,3,1:T(4,128)(2,1)}), bf16[4,8,4,4,128]{4,0,2,3,1:T(4,128)(2,1)S(1)}, u32[]{:S(2)}, u32[]{:S(2)}) async-start(bf16[4,8,4,4,128]{4,0,2,3,1:T(4,128)(2,1)} %copy.61), calls=%async_computation.2 | async-start | bytes 262144 | tf_op jit(solution)/shard_map/all_to_all | solution.py:59
  98.6 35.1 %reduce-scatter.7.cloned.1.call-start = ((), (), s32[]{:S(2)}) async-start(), calls=%async_computation.7 | async-start | bytes 1572864
Sparse Core Ops, SparseCore 0:
  8.9 26.8 all-gather.1
  44.6 23.6 all-reduce.1
  80.6 11.6 reduce-scatter.4
  115.3 18.3 reduce-scatter.6

commit v2 on v1

--- a/solution.py
+++ b/solution.py
@@ -3,6 +3,8 @@
 import jax
 import jax.numpy as jnp
 from jax import lax
+from jax.experimental import pallas as pl
+from jax.experimental.pallas import tpu as pltpu
 from jax.sharding import PartitionSpec as P
 
 HD = 128
@@ -21,7 +23,7 @@
     return jnp.sum(picked * slot_of[None, :], axis=1)
 
 
-def on_device(kv_rows, basis, out_weight, queries, new_kv, owner, req_start):
+def by_collectives(kv_rows, basis, out_weight, queries, new_kv, owner, req_start):
     owners = lax.axis_size("ctx") * lax.axis_size("dp")
     rows, feat = kv_rows.shape
     own_slots, local_j, half = queries.shape
@@ -78,6 +80,365 @@
     out = jnp.dot(att, out_weight, preferred_element_type=f32)
     return lax.psum_scatter(out.astype(bf16), "tp", scatter_dimension=1, tiled=True)
 
+NT = (((1,), (1,)), ((), ()))
+NN = (((1,), (0,)), ((), ()))
+LOW = -1e30
+CHUNKS = 4
+
+
+def dot(a, b, dims=NN):
+    return lax.dot_general(a, b, dims, preferred_element_type=jnp.float32)
+
+
+def roll4(x):
+    return pltpu.roll(x, 4, 0)
+
+
+def handoff_kernel(
+    owner_ref, start_ref, q_ref, new_ref, basis_ref, kv_hbm, w_hbm, out_ref,
+    kv, w, qbuf, bbuf, gram_k, gram_v, qf, slotm_ref, ssend, srecv, sdup, p_scr, tops,
+    pblk, asend, arecv, tsend, trecv, x16, osend, orecv,
+    loc_sem, q1_sem, qs_sem, qr_sem, b_sem, s_sem, r_sem, as_sem, ar_sem, ts_sem, tr_sem, o_sem,
+):
+    f32, bf16, i32 = jnp.float32, jnp.bfloat16, jnp.int32
+    owners = qbuf.shape[0]
+    slots = 4 * owners
+    rows = kv.shape[0]
+    cn = rows // CHUNKS
+    scale = 1.0 / math.sqrt(HD)
+    dp, tp = lax.axis_index("dp"), lax.axis_index("tp")
+    me = lax.axis_index("ctx") * 2 + dp
+    oth = 1 - tp
+    half_cols = w.shape[2]
+
+    def at(o, t):
+        return {"ctx": o // 2, "dp": lax.rem(o, 2), "tp": t}
+
+    def remote(src, dst, ssem, rsem, o, t):
+        return pltpu.make_async_remote_copy(
+            src_ref=src, dst_ref=dst, send_sem=ssem, recv_sem=rsem,
+            device_id=at(o, t), device_id_type=pl.DeviceIdType.MESH,
+        )
+
+    kv_copy = pltpu.make_async_copy(kv_hbm, kv, loc_sem.at[0])
+    kv_copy.start()
+    w_copies = []
+    for h, side in enumerate((oth, tp)):
+        cols = pl.ds(pl.multiple_of(side * half_cols, half_cols), half_cols)
+        w_copies.append(pltpu.make_async_copy(w_hbm.at[:, cols], w.at[h], loc_sem.at[1 + h]))
+        w_copies[-1].start()
+
+    barrier = pltpu.get_barrier_semaphore()
+
+    def greet(i, c):
+        o = lax.rem(me + i, owners)
+        for t in range(2):
+            pl.semaphore_signal(barrier, inc=1, device_id=at(o, t), device_id_type=pl.DeviceIdType.MESH)
+        return c
+
+    lax.fori_loop(1, owners, greet, 0)
+    pl.semaphore_signal(barrier, inc=1, device_id=at(me, oth), device_id_type=pl.DeviceIdType.MESH)
+    pl.semaphore_wait(barrier, 2 * owners - 1)
+
+    q1 = remote(q_ref, qbuf.at[me, tp], q1_sem.at[0], q1_sem.at[1], me, oth)
+    q1.start()
+    hb = bbuf.shape[2]
+    b1 = remote(
+        basis_ref.at[pl.ds(pl.multiple_of(dp * hb, hb), hb)], bbuf.at[tp, dp],
+        b_sem.at[0], b_sem.at[1], me, oth,
+    )
+    b1.start()
+    qbuf[me, tp] = q_ref[...]
+    q1.wait()
+
+    def q_copy(o, src):
+        return remote(qbuf.at[me], qbuf.at[src], qs_sem.at[o], qr_sem.at[src], o, tp)
+
+    def q_start(i, c):
+        q_copy(lax.rem(me + i, owners), me).start()
+        return c
+
+    lax.fori_loop(1, owners, q_start, 0)
+
+    bbuf[tp, 0] = basis_ref[:hb]
+    bbuf[tp, 1] = basis_ref[hb:]
+    req = owner_ref.shape[1]
+    ri = lax.broadcasted_iota(i32, (req, req), 0)
+    ci = lax.broadcasted_iota(i32, (req, req), 1)
+
+    def column(row, shift=0):
+        return jnp.sum(jnp.where(ci == ri + shift, jnp.broadcast_to(row, (req, req)), 0), axis=1, keepdims=True)
+
+    own_row = owner_ref[...]
+    own_col = column(own_row)
+    same = (own_row == own_col) & (ci < ri)
+    slot_col = own_col * 4 + jnp.sum(jnp.where(same, 1, 0), axis=1, keepdims=True)
+    first = column(start_ref[...])
+    rc = lax.broadcasted_iota(i32, (req, 1), 0)
+    last = column(start_ref[...], 1) + jnp.where(rc == req - 1, rows, 0)
+    tok = lax.broadcasted_iota(i32, (req, rows), 1)
+    slot = jnp.sum(jnp.where((tok >= first) & (tok < last), slot_col, 0), axis=0, keepdims=True)
+    slotm_ref[...] = jnp.broadcast_to(slot, (8, rows)) - lax.broadcasted_iota(i32, (8, rows), 0) // 4
+
+    lane_g = lax.broadcasted_iota(i32, (16, 128), 1) // 32
+    row_k = lax.broadcasted_iota(i32, (16, 1), 0) // 4
+    fresh = jnp.zeros((16, 1024), f32)
+    for k in range(4):
+        fresh = jnp.where(row_k == k, new_ref[k : k + 1, :].astype(f32), fresh)
+    qk = q_ref[...].astype(f32) * fresh[:, :512]
+    own = jnp.zeros((16, 128), f32)
+    for g in range(4):
+        s = jnp.sum(qk[:, g * HD : (g + 1) * HD], axis=1, keepdims=True) * scale
+        own = jnp.where(lane_g == g, s, own)
+
+    b1.wait()
+    sib = 2 * lax.axis_index("ctx") + 1 - dp
+    b2 = remote(bbuf.at[oth, dp], bbuf.at[oth, dp], b_sem.at[2], b_sem.at[3], sib, tp)
+    b2.start()
+    b2.wait()
+    full_k = bbuf[0].reshape(512, 512)
+    full_v = bbuf[1].reshape(512, 512)
+    gram_k[...] = dot(full_k, basis_ref[...], NT).astype(bf16)
+    gram_v[...] = dot(basis_ref[...], full_v, NT).astype(bf16)
+
+    def q_wait(i, c):
+        o = lax.rem(me + i, owners)
+        cp = q_copy(o, o)
+        cp.wait_recv()
+        q_copy(o, me).wait_send()
+        return c
+
+    lax.fori_loop(1, owners, q_wait, 0)
+    q_rows = qbuf[...].reshape(slots * 8, 512)
+    for g in range(4):
+        qf[g] = dot(q_rows[:, g * HD : (g + 1) * HD], gram_k[g * HD : (g + 1) * HD, :]).astype(bf16)
+    kv_copy.wait()
+
+    low8 = lax.broadcasted_iota(i32, (8, cn), 0) < 4
+
+    def s_copy(c):
+        return remote(ssend.at[c], srecv.at[c], s_sem.at[c], r_sem.at[c], me, oth)
+
+    def score_chunk(c, carry):
+        span = pl.ds(pl.multiple_of(c * cn, cn), cn)
+        kvc = kv[span, :]
+        sm = slotm_ref[:, span]
+        for g in range(4):
+            dense = dot(qf[g], kvc, NT)
+            folded = []
+            for t in range(2):
+                acc = jnp.zeros((8, cn), f32)
+                for o in range(owners):
+                    for k2 in range(2):
+                        r0 = o * 32 + t * 16 + k2 * 8
+                        acc = jnp.where(sm == o * 4 + 2 * k2, dense[r0 : r0 + 8], acc)
+                folded.append(acc)
+            folded = [a + roll4(a) for a in folded]
+            ssend[c, g * 8 : (g + 1) * 8, :] = jnp.where(low8, folded[0], folded[1])
+        s_copy(c).start()
+        return carry
+
+    lax.fori_loop(0, CHUNKS, score_chunk, 0)
+
+    def merge_chunk(c, carry):
+        span = pl.ds(pl.multiple_of(c * cn, cn), cn)
+        s_copy(c).wait()
+        for g in range(4):
+            part = (ssend[c, g * 8 : (g + 1) * 8, :] + srecv[c, g * 8 : (g + 1) * 8, :]) * scale
+            turned = roll4(part)
+            sdup[2 * g, :, span] = jnp.where(low8, part, turned)
+            sdup[2 * g + 1, :, span] = jnp.where(low8, turned, part)
+        return carry
+
+    lax.fori_loop(0, CHUNKS, merge_chunk, 0)
+
+    def soft(gt, carry):
+        s = sdup[gt]
+        sm = slotm_ref[...]
+        top_tok = jnp.zeros((8, rows), f32)
+        for c in range(2 * owners):
+            live = sm == 2 * c
+            top = jnp.max(jnp.where(live, s, LOW), axis=1, keepdims=True)
+            tops[c, gt] = jnp.broadcast_to(top, (8, 128))
+            top_tok = jnp.where(live, top, top_tok)
+        top_tok = top_tok + roll4(top_tok)
+        p_scr[gt] = jnp.exp(s - top_tok)
+        return carry
+
+    lax.fori_loop(0, 8, soft, 0)
+
+    def a_copies(o, so):
+        return [
+            remote(asend.at[o * 2 + t], arecv.at[so * 2 + tp], as_sem.at[o * 2 + t], ar_sem.at[so * 2 + tp], o, t)
+            for t in range(2)
+        ]
+
+    def t_copy(o, so):
+        return remote(tsend.at[o], trecv.at[so], ts_sem.at[o], tr_sem.at[so], o, tp)
+
+    def share(o):
+        sm = slotm_ref[...]
+        tot = []
+        for gt in range(8):
+            p = p_scr[gt]
+            tiles = [jnp.where(sm == o * 4 + 2 * k2, p, 0.0) for k2 in range(2)]
+            both = jnp.concatenate(tiles, axis=0)
+            tot.append(jnp.sum(both, axis=1, keepdims=True))
+            pblk[gt * 16 : (gt + 1) * 16, :] = both.astype(bf16)
+        u = dot(pblk[...], kv[...]).astype(bf16)
+        stat = jnp.full((16, 128), LOW, f32)
+        for g in range(4):
+            a = dot(u[g * 32 : (g + 1) * 32], gram_v[:, g * HD : (g + 1) * HD])
+            lse = []
+            for t in range(2):
+                l = tot[2 * g + t]
+                inv = 1.0 / jnp.where(l > 0.0, l, 1.0)
+                asend[o * 2 + t, :, g * HD : (g + 1) * HD] = (a[t * 16 : (t + 1) * 16] * inv).astype(bf16)
+                top = jnp.concatenate([tops[2 * o, 2 * g + t], tops[2 * o + 1, 2 * g + t]], axis=0)
+                lse.append(jnp.where(l > 0.0, top + jnp.log(jnp.where(l > 0.0, l, 1.0)), LOW))
+            stat = jnp.where(lane_g == g, jnp.where(tp == 0, lse[0], lse[1]), stat)
+        tsend[o] = stat
+
+    def share_send(i, carry):
+        o = lax.rem(me + i, owners)
+        share(o)
+        for cp in a_copies(o, me):
+            cp.start()
+        t_copy(o, me).start()
+        return carry
+
+    lax.fori_loop(1, owners, share_send, 0)
+    share(me)
+    pair = remote(
+        asend.at[me * 2 + oth], arecv.at[me * 2 + tp], as_sem.at[me * 2 + oth], ar_sem.at[me * 2 + tp], me, oth
+    )
+    pair.start()
+    arecv[me * 2 + tp] = asend[me * 2 + tp]
+    trecv[me] = tsend[me]
+
+    def share_wait(i, carry):
+        o = lax.rem(me + i, owners)
+        for cp in a_copies(o, me):
+            cp.wait_send()
+        t_copy(o, me).wait_send()
+        for t in range(2):
+            remote(
+                asend.at[o * 2 + t], arecv.at[o * 2 + t], as_sem.at[o * 2 + t], ar_sem.at[o * 2 + t], o, t
+            ).wait_recv()
+        t_copy(o, o).wait_recv()
+        return carry
+
+    lax.fori_loop(1, owners, share_wait, 0)
+    pair.wait_send()
+    remote(
+        asend.at[me * 2 + oth], arecv.at[me * 2 + oth], as_sem.at[me * 2 + oth], ar_sem.at[me * 2 + oth], me, oth
+    ).wait_recv()
+
+    best = own
+    for s in range(owners):
+        best = jnp.maximum(best, trecv[s])
+    own_w = jnp.exp(own - best)
+    denom = own_w
+    lifts = []
+    for s in range(owners):
+        lifts.append(jnp.exp(trecv[s] - best))
+        denom = denom + lifts[-1]
+    inv = 1.0 / denom
+    row_j = lax.rem(lax.broadcasted_iota(i32, (16, 1), 0), 4)
+    fold = jnp.where(
+        lax.broadcasted_iota(i32, (16, 16), 1) // 4 == lax.rem(lax.broadcasted_iota(i32, (16, 16), 0), 4), 1.0, 0.0
+    ).astype(bf16)
+    for g in range(4):
+        cols = slice(g * HD, (g + 1) * HD)
+        att = own_w[:, 32 * g : 32 * g + 1] * fresh[:, 512 + g * HD : 512 + (g + 1) * HD]
+        for s in range(owners):
+            both = arecv[2 * s, :, cols].astype(f32) + arecv[2 * s + 1, :, cols].astype(f32)
+            att = att + lifts[s][:, 32 * g : 32 * g + 1] * both
+        att = att * inv[:, 32 * g : 32 * g + 1]
+        for j in range(4):
+            pick = jnp.where(row_j == j, att, 0.0).astype(bf16)
+            x16[:, j * 512 + g * HD : j * 512 + (g + 1) * HD] = dot(fold, pick).astype(bf16)
+
+    o_copy = remote(osend, orecv, o_sem.at[0], o_sem.at[1], me, oth)
+    quarter = half_cols // 2
+    lowq = lax.broadcasted_iota(i32, (8, 256), 0) < 4
+    for h in range(2):
+        w_copies[h].wait()
+
+        def column_tile(j, carry, h=h):
+            left = pl.ds(pl.multiple_of(j * 256, 256), 256)
+            right = pl.ds(pl.multiple_of(quarter + j * 256, 256), 256)
+            a = dot(x16[...], w[h, :, left])
+            b = dot(x16[...], w[h, :, right])
+            picked = jnp.where(lowq, a[:8], b[:8])
+            if h == 0:
+                osend[:, left] = picked
+            else:
+                out_ref[:, left] = picked
+            return carry
+
+        lax.fori_loop(0, quarter // 256, column_tile, 0)
+        if h == 0:
+            o_copy.start()
+    o_copy.wait()
+    out_ref[...] = out_ref[...] + orecv[...]
+
+
+def fused(kv_rows, basis, out_weight, queries, new_kv, owner, req_start):
+    f32, bf16 = jnp.float32, jnp.bfloat16
+    owners = lax.axis_size("ctx") * lax.axis_size("dp")
+    rows = kv_rows.shape[0]
+    slots = owners * 4
+    half_cols = out_weight.shape[1] // 2
+    dma = pltpu.SemaphoreType.DMA
+    vm = pl.BlockSpec(memory_space=pltpu.VMEM)
+    hbm = pl.BlockSpec(memory_space=pl.ANY)
+    out = pl.pallas_call(
+        handoff_kernel,
+        out_shape=jax.ShapeDtypeStruct((8, half_cols // 2), f32),
+        in_specs=[vm, vm, vm, vm, vm, hbm, hbm],
+        out_specs=vm,
+        scratch_shapes=[
+            pltpu.VMEM((rows, 512), bf16),
+            pltpu.VMEM((2, out_weight.shape[0], half_cols), bf16),
+            pltpu.VMEM((owners, 2, 16, 512), bf16),
+            pltpu.VMEM((2, 2, 256, 512), bf16),
+            pltpu.VMEM((512, 512), bf16),
+            pltpu.VMEM((512, 512), bf16),
+            pltpu.VMEM((4, slots * 8, 512), bf16),
+            pltpu.VMEM((8, rows), jnp.int32),
+            pltpu.VMEM((CHUNKS, 32, rows // CHUNKS), f32),
+            pltpu.VMEM((CHUNKS, 32, rows // CHUNKS), f32),
+            pltpu.VMEM((8, 8, rows), f32),
+            pltpu.VMEM((8, 8, rows), f32),
+            pltpu.VMEM((2 * owners, 8, 8, 128), f32),
+            pltpu.VMEM((128, rows), bf16),
+            pltpu.VMEM((2 * owners, 16, 512), bf16),
+            pltpu.VMEM((2 * owners, 16, 512), bf16),
+            pltpu.VMEM((owners, 16, 128), f32),
+            pltpu.VMEM((owners, 16, 128), f32),
+            pltpu.VMEM((16, out_weight.shape[0]), bf16),
+            pltpu.VMEM((8, half_cols // 2), f32),
+            pltpu.VMEM((8, half_cols // 2), f32),
+            dma((3,)), dma((2,)), dma((owners,)), dma((owners,)), dma((4,)),
+            dma((CHUNKS,)), dma((CHUNKS,)),
+            dma((2 * owners,)), dma((2 * owners,)), dma((owners,)), dma((owners,)), dma((2,)),
+        ],
+        compiler_params=pltpu.CompilerParams(
+            collective_id=0, has_side_effects=True, vmem_limit_bytes=56 * 1024 * 1024
+        ),
+    )(
+        owner.reshape(1, -1), req_start, queries.reshape(16, 512), new_kv, basis, kv_rows, out_weight,
+    )
+    return jnp.concatenate([out[:4], out[4:]], axis=1).astype(bf16)
+
+
+def on_device(kv_rows, basis, out_weight, queries, new_kv, owner, req_start):
+    args = (kv_rows, basis, out_weight, queries, new_kv, owner, req_start)
+    if queries.shape == (4, 4, 512) and lax.axis_size("tp") == 2 and lax.axis_size("dp") == 2:
+        return fused(*args)
+    return by_collectives(*args)
+
 
 def solution(mesh):
     return jax.shard_map(

time: 143 us -> 45.5 us (0.32)
  waiting for transfers between devices: 54.5 us -> 0 us
  Pallas kernels: 0 us -> 42.6 us
  blocking collectives: 25.5 us -> 0 us
  matrix products: 21.9 us -> 0 us
  between operations: 13.3 us -> 0.01 us
  starting transfers between devices: 8.29 us -> 0 us
  other arithmetic: 9.44 us -> 1.38 us
  local copies, waits for them, and re-layouts: 9.22 us -> 1.34 us
    pallas_call x0 -> x1, Pallas kernels: none -> 42.6 us  [fused(): pl.pallas_call(handoff_kernel, out_shape=jax.ShapeDtypeStruct((8, half_co...]
    all_gather x2 -> x0, blocking collectives: 25.5 us -> none  [the longest x1 15.9 us: on_device(): q_all = lax.all_gather(queries, ('ctx', 'dp'), axis=0, tiled=True)]
    psum x1 -> x0, waiting for transfers between devices: 23.8 us -> none  [on_device(): score = lax.psum(part, 'tp') * scale]
    dot_general x6 -> x0, matrix products: 21.9 us -> none  [the longest x1 8.04 us: on_device(): out = jnp.dot(att, out_weight, preferred_element_type=f32)]
    unnamed x5 -> x0, waiting for transfers between devices: 19.3 us -> none
    all_to_all x2 -> x0, waiting for transfers between devices: 11.1 us -> none  [the longest x1 6.42 us: on_device(): lax.all_to_all(mixed.reshape(local_j, owners, own_slots, groups, HD), ('c...]
    all_to_all x2 -> x0, starting transfers between devices: 7.98 us -> none  [the longest x1 4.61 us: on_device(): lax.all_to_all(stats.reshape(local_j, owners, own_slots, groups, 2), ('ct...]
    reduce_sum x7 -> x0, other arithmetic: 4.77 us -> none  [the longest x1 1.7 us: on_device(): total = jnp.sum(spread, axis=3)]
  transfers between devices with their start and end apart: 6 -> 0, of which waited for: 5 -> 0; matrix products, arithmetic and copies ran while one was open for 5% -> 0% of each run, Pallas kernels for 0% -> 0%
where the time goes in v2:
time: 45.5 us; the launch traced here: 45.3 us
  Pallas kernels  42.6 us (94%)
  other arithmetic  1.38 us (3%)
  local copies, waits for them, and re-layouts  1.34 us (3%)
    pallas_call x1, Pallas kernels, fused(): pl.pallas_call(handoff_kernel, out_shape=jax.ShapeDtypeStruct((8, half_co...  42.6 us
    reshape x1, local copies, waits for them, and re-layouts, fused(): queries.reshape(16, 512)  1.33 us

profile of v2, /device:TPU:0, one launch (start us, length us, event | category | flops | bytes accessed | tf_op | source)
XLA Modules:
  0.0 45.3 jit_solution(6150922394133187675)
XLA Ops:
  0.0 1.3 %reshape.7.q_ref = bf16[16,512]{1,0:T(8,128)(2,1)} reshape(bf16[4,4,512]{2,1,0:T(4,128)(2,1)} %param.10) | data formatting | bytes 32768 | tf_op jit(solution)/shard_map/reshape | solution.py:431
  1.3 42.6 %shard_map.73 = f32[8,1024]{1,0:T(8,128)} custom-call(s32[1,32]{1,0:T(1,128)} %bitcast.1, s32[1,32]{1,0:T(1,128)} %start_ref.1, bf16[16,512]{1,0:T(8,128)(2,1)} %reshape.7.q_ref, bf16[4,1024]{1,0:T(4,128)(2,1)} %new_ref.1, bf16[512,512]{1,0:T(8,128)(2,1)} %basis_ref.1, bf16[2048,512]{1,0:T(8,128)(2,1)} %kv_hbm.1, bf16[2048,4096]{1,0:T(8,128)(2,1)} %w_hbm.1), custom_call_target="tpu_custom_call" | custom-call | tf_op jit(solution)/shard_map/pallas_call | solution.py:396
  43.9 0.8 %convert.6 = bf16[8,1024]{1,0:T(8,128)(2,1)S(1)} convert(f32[8,1024]{1,0:T(8,128)} %shard_map.73) | non-fusion elementwise | flops 8192 | bytes 49152 | tf_op jit(solution)/shard_map/convert.3
  44.7 0.6 %pad_maximum_fusion = bf16[4,2048]{1,0:T(4,128)(2,1)} fusion(bf16[4,1024]{1,0:T(4,128)(2,1)S(1)} %get-tuple-element.6, bf16[4,1024]{1,0:T(4,128)(2,1)S(1)} %get-tuple-element.5), kind=kLoop, calls=%fused_computation | loop fusion | flops 32768 | bytes 32768 | tf_op jit(solution)/shard_map/concatenate | solution.py:433
  (1 shorter events, 0.0 us)

commit v3 on v2

--- a/solution.py
+++ b/solution.py
@@ -95,9 +95,9 @@
 
 
 def handoff_kernel(
-    owner_ref, start_ref, q_ref, new_ref, basis_ref, kv_hbm, w_hbm, out_ref,
-    kv, w, qbuf, bbuf, gram_k, gram_v, qf, slotm_ref, ssend, srecv, sdup, p_scr, tops,
-    pblk, asend, arecv, tsend, trecv, x16, osend, orecv,
+    owner_ref, start_ref, q3_ref, new_ref, basis_ref, kv_hbm, w_hbm, out_ref,
+    kv, w, q_ref, qbuf, bbuf, gram_k, gram_v, qf, slotm_ref, mine, ssend, srecv, sdup, p_scr, tops,
+    pblk, asend, arecv, tsend, trecv, x16, osend, orecv, outf,
     loc_sem, q1_sem, qs_sem, qr_sem, b_sem, s_sem, r_sem, as_sem, ar_sem, ts_sem, tr_sem, o_sem,
 ):
     f32, bf16, i32 = jnp.float32, jnp.bfloat16, jnp.int32
@@ -128,6 +128,7 @@
         w_copies.append(pltpu.make_async_copy(w_hbm.at[:, cols], w.at[h], loc_sem.at[1 + h]))
         w_copies[-1].start()
 
+    q_ref[...] = jnp.concatenate([q3_ref[k].astype(f32) for k in range(4)], axis=0).astype(bf16)
     barrier = pltpu.get_barrier_semaphore()
 
     def greet(i, c):
@@ -180,6 +181,7 @@
     slot = jnp.sum(jnp.where((tok >= first) & (tok < last), slot_col, 0), axis=0, keepdims=True)
     slotm_ref[...] = jnp.broadcast_to(slot, (8, rows)) - lax.broadcasted_iota(i32, (8, rows), 0) // 4
 
+    low_lane = lax.rem(lax.broadcasted_iota(i32, (8, 128), 1), 32) < 16
     lane_g = lax.broadcasted_iota(i32, (16, 128), 1) // 32
     row_k = lax.broadcasted_iota(i32, (16, 1), 0) // 4
     fresh = jnp.zeros((16, 1024), f32)
@@ -223,6 +225,7 @@
         span = pl.ds(pl.multiple_of(c * cn, cn), cn)
         kvc = kv[span, :]
         sm = slotm_ref[:, span]
+        parts = []
         for g in range(4):
             dense = dot(qf[g], kvc, NT)
             folded = []
@@ -234,7 +237,10 @@
                         acc = jnp.where(sm == o * 4 + 2 * k2, dense[r0 : r0 + 8], acc)
                 folded.append(acc)
             folded = [a + roll4(a) for a in folded]
-            ssend[c, g * 8 : (g + 1) * 8, :] = jnp.where(low8, folded[0], folded[1])
+            parts.append(jnp.where(low8, folded[0], folded[1]))
+        parts = jnp.concatenate(parts, axis=0)
+        mine[c] = parts
+        ssend[c] = parts.astype(bf16)
         s_copy(c).start()
         return carry
 
@@ -243,8 +249,9 @@
     def merge_chunk(c, carry):
         span = pl.ds(pl.multiple_of(c * cn, cn), cn)
         s_copy(c).wait()
+        both = (mine[c] + srecv[c].astype(f32)) * scale
         for g in range(4):
-            part = (ssend[c, g * 8 : (g + 1) * 8, :] + srecv[c, g * 8 : (g + 1) * 8, :]) * scale
+            part = both[g * 8 : (g + 1) * 8]
             turned = roll4(part)
             sdup[2 * g, :, span] = jnp.where(low8, part, turned)
             sdup[2 * g + 1, :, span] = jnp.where(low8, turned, part)
@@ -276,39 +283,53 @@
     def t_copy(o, so):
         return remote(tsend.at[o], trecv.at[so], ts_sem.at[o], tr_sem.at[so], o, tp)
 
-    def share(o):
+    def share(ctx):
         sm = slotm_ref[...]
         tot = []
-        for gt in range(8):
-            p = p_scr[gt]
-            tiles = [jnp.where(sm == o * 4 + 2 * k2, p, 0.0) for k2 in range(2)]
-            both = jnp.concatenate(tiles, axis=0)
-            tot.append(jnp.sum(both, axis=1, keepdims=True))
-            pblk[gt * 16 : (gt + 1) * 16, :] = both.astype(bf16)
+        for d in range(2):
+            for gt in range(8):
+                p = p_scr[gt]
+                tiles = [jnp.where(sm == ctx * 8 + d * 4 + 2 * k2, p, 0.0) for k2 in range(2)]
+                both = jnp.concatenate(tiles, axis=0)
+                tot.append(jnp.sum(both, axis=1, keepdims=True))
+                r0 = d * 128 + gt * 16
+                pblk[r0 : r0 + 16, :] = both.astype(bf16)
         u = dot(pblk[...], kv[...]).astype(bf16)
-        stat = jnp.full((16, 128), LOW, f32)
+        stats = [jnp.full((16, 128), LOW, f32) for _ in range(2)]
         for g in range(4):
-            a = dot(u[g * 32 : (g + 1) * 32], gram_v[:, g * HD : (g + 1) * HD])
-            lse = []
-            for t in range(2):
-                l = tot[2 * g + t]
-                inv = 1.0 / jnp.where(l > 0.0, l, 1.0)
-                asend[o * 2 + t, :, g * HD : (g + 1) * HD] = (a[t * 16 : (t + 1) * 16] * inv).astype(bf16)
-                top = jnp.concatenate([tops[2 * o, 2 * g + t], tops[2 * o + 1, 2 * g + t]], axis=0)
-                lse.append(jnp.where(l > 0.0, top + jnp.log(jnp.where(l > 0.0, l, 1.0)), LOW))
-            stat = jnp.where(lane_g == g, jnp.where(tp == 0, lse[0], lse[1]), stat)
-        tsend[o] = stat
-
-    def share_send(i, carry):
-        o = lax.rem(me + i, owners)
-        share(o)
+            rows_g = jnp.concatenate([u[d * 128 + g * 32 : d * 128 + (g + 1) * 32] for d in range(2)], axis=0)
+            a = dot(rows_g, gram_v[:, g * HD : (g + 1) * HD])
+            for d in range(2):
+                o = ctx * 2 + d
+                lse = []
+                for t in range(2):
+                    l = tot[d * 8 + 2 * g + t]
+                    inv = 1.0 / jnp.where(l > 0.0, l, 1.0)
+                    r0 = d * 32 + t * 16
+                    asend[o * 2 + t, :, g * HD : (g + 1) * HD] = (a[r0 : r0 + 16] * inv).astype(bf16)
+                    top = jnp.concatenate([tops[2 * o, 2 * g + t], tops[2 * o + 1, 2 * g + t]], axis=0)
+                    lse.append(jnp.where(l > 0.0, top + jnp.log(jnp.where(l > 0.0, l, 1.0)), LOW))
+                stats[d] = jnp.where(lane_g == g, jnp.where(tp == 0, lse[0], lse[1]), stats[d])
+        for d in range(2):
+            tsend[ctx * 2 + d] = jnp.where(low_lane, stats[d][:8], stats[d][8:])
+
+    my_ctx = lax.axis_index("ctx")
+
+    def send_all(o):
         for cp in a_copies(o, me):
             cp.start()
         t_copy(o, me).start()
+
+    def share_send(i, carry):
+        c = lax.rem(my_ctx + i, owners // 2)
+        share(c)
+        for d in range(2):
+            send_all(c * 2 + d)
         return carry
 
-    lax.fori_loop(1, owners, share_send, 0)
-    share(me)
+    lax.fori_loop(1, owners // 2, share_send, 0)
+    share(my_ctx)
+    send_all(sib)
     pair = remote(
         asend.at[me * 2 + oth], arecv.at[me * 2 + tp], as_sem.at[me * 2 + oth], ar_sem.at[me * 2 + tp], me, oth
     )
@@ -334,6 +355,7 @@
         asend.at[me * 2 + oth], arecv.at[me * 2 + oth], as_sem.at[me * 2 + oth], ar_sem.at[me * 2 + oth], me, oth
     ).wait_recv()
 
+    own = jnp.where(low_lane, own[:8], own[8:])
     best = own
     for s in range(owners):
         best = jnp.maximum(best, trecv[s])
@@ -344,17 +366,21 @@
         lifts.append(jnp.exp(trecv[s] - best))
         denom = denom + lifts[-1]
     inv = 1.0 / denom
+
+    def spread(x, g):
+        return jnp.concatenate([x[:, 32 * g : 32 * g + 1], x[:, 32 * g + 16 : 32 * g + 17]], axis=0)
+
     row_j = lax.rem(lax.broadcasted_iota(i32, (16, 1), 0), 4)
     fold = jnp.where(
         lax.broadcasted_iota(i32, (16, 16), 1) // 4 == lax.rem(lax.broadcasted_iota(i32, (16, 16), 0), 4), 1.0, 0.0
     ).astype(bf16)
     for g in range(4):
         cols = slice(g * HD, (g + 1) * HD)
-        att = own_w[:, 32 * g : 32 * g + 1] * fresh[:, 512 + g * HD : 512 + (g + 1) * HD]
+        att = spread(own_w, g) * fresh[:, 512 + g * HD : 512 + (g + 1) * HD]
         for s in range(owners):
             both = arecv[2 * s, :, cols].astype(f32) + arecv[2 * s + 1, :, cols].astype(f32)
-            att = att + lifts[s][:, 32 * g : 32 * g + 1] * both
-        att = att * inv[:, 32 * g : 32 * g + 1]
+            att = att + spread(lifts[s], g) * both
+        att = att * spread(inv, g)
         for j in range(4):
             pick = jnp.where(row_j == j, att, 0.0).astype(bf16)
             x16[:, j * 512 + g * HD : j * 512 + (g + 1) * HD] = dot(fold, pick).astype(bf16)
@@ -374,14 +400,16 @@
             if h == 0:
                 osend[:, left] = picked
             else:
-                out_ref[:, left] = picked
+                outf[:, left] = picked
             return carry
 
         lax.fori_loop(0, quarter // 256, column_tile, 0)
         if h == 0:
             o_copy.start()
     o_copy.wait()
-    out_ref[...] = out_ref[...] + orecv[...]
+    total = outf[...] + orecv[...]
+    out_ref[:, :quarter] = total[:4].astype(bf16)
+    out_ref[:, quarter:] = roll4(total)[:4].astype(bf16)
 
 
 def fused(kv_rows, basis, out_weight, queries, new_kv, owner, req_start):
@@ -395,12 +423,13 @@
     hbm = pl.BlockSpec(memory_space=pl.ANY)
     out = pl.pallas_call(
         handoff_kernel,
-        out_shape=jax.ShapeDtypeStruct((8, half_cols // 2), f32),
+        out_shape=jax.ShapeDtypeStruct((4, half_cols), bf16),
         in_specs=[vm, vm, vm, vm, vm, hbm, hbm],
         out_specs=vm,
         scratch_shapes=[
             pltpu.VMEM((rows, 512), bf16),
             pltpu.VMEM((2, out_weight.shape[0], half_cols), bf16),
+            pltpu.VMEM((16, 512), bf16),
             pltpu.VMEM((owners, 2, 16, 512), bf16),
             pltpu.VMEM((2, 2, 256, 512), bf16),
             pltpu.VMEM((512, 512), bf16),
@@ -408,16 +437,18 @@
             pltpu.VMEM((4, slots * 8, 512), bf16),
             pltpu.VMEM((8, rows), jnp.int32),
             pltpu.VMEM((CHUNKS, 32, rows // CHUNKS), f32),
-            pltpu.VMEM((CHUNKS, 32, rows // CHUNKS), f32),
+            pltpu.VMEM((CHUNKS, 32, rows // CHUNKS), bf16),
+            pltpu.VMEM((CHUNKS, 32, rows // CHUNKS), bf16),
             pltpu.VMEM((8, 8, rows), f32),
             pltpu.VMEM((8, 8, rows), f32),
             pltpu.VMEM((2 * owners, 8, 8, 128), f32),
-            pltpu.VMEM((128, rows), bf16),
+            pltpu.VMEM((256, rows), bf16),
             pltpu.VMEM((2 * owners, 16, 512), bf16),
             pltpu.VMEM((2 * owners, 16, 512), bf16),
-            pltpu.VMEM((owners, 16, 128), f32),
-            pltpu.VMEM((owners, 16, 128), f32),
+            pltpu.VMEM((owners, 8, 128), f32),
+            pltpu.VMEM((owners, 8, 128), f32),
             pltpu.VMEM((16, out_weight.shape[0]), bf16),
+            pltpu.VMEM((8, half_cols // 2), f32),
             pltpu.VMEM((8, half_cols // 2), f32),
             pltpu.VMEM((8, half_cols // 2), f32),
             dma((3,)), dma((2,)), dma((owners,)), dma((owners,)), dma((4,)),
@@ -428,9 +459,9 @@
             collective_id=0, has_side_effects=True, vmem_limit_bytes=56 * 1024 * 1024
         ),
     )(
-        owner.reshape(1, -1), req_start, queries.reshape(16, 512), new_kv, basis, kv_rows, out_weight,
+        owner.reshape(1, -1), req_start, queries, new_kv, basis, kv_rows, out_weight,
     )
-    return jnp.concatenate([out[:4], out[4:]], axis=1).astype(bf16)
+    return out
 
 
 def on_device(kv_rows, basis, out_weight, queries, new_kv, owner, req_start):

time: 45.5 us -> 40.6 us (0.89)
  Pallas kernels: 42.6 us -> 39 us
  other arithmetic: 1.38 us -> 0 us
    pallas_call x1, Pallas kernels: 42.6 us -> 39 us  [fused(): pl.pallas_call(handoff_kernel, out_shape=jax.ShapeDtypeStruct((4, half_co...]
    reshape x1 -> x0, local copies, waits for them, and re-layouts: 1.33 us -> none  [fused(): queries.reshape(16, 512)]
    unnamed x0 -> x1, local copies, waits for them, and re-layouts: none -> 1.33 us
    another operation x1 -> x0, other arithmetic: 0.76 us -> none
    concatenate x1 -> x0, other arithmetic: 0.62 us -> none  [fused(): return jnp.concatenate([out[:4], out[4:]], axis=1).astype(bf16)]
where the time goes in v3:
time: 40.6 us; the launch traced here: 40.3 us
  Pallas kernels  39 us (96%)
  local copies, waits for them, and re-layouts  1.33 us (3%)
    pallas_call x1, Pallas kernels, fused(): pl.pallas_call(handoff_kernel, out_shape=jax.ShapeDtypeStruct((4, half_co...  39 us
    unnamed x1, local copies, waits for them, and re-layouts  1.33 us

profile of v3, /device:TPU:0, one launch (start us, length us, event | category | flops | bytes accessed | tf_op | source)
XLA Modules:
  0.0 40.3 jit_solution(6701654609692499224)
XLA Ops:
  0.0 39.0 %shard_map.73 = bf16[4,2048]{1,0:T(4,128)(2,1)} custom-call(s32[1,32]{1,0:T(1,128)} %bitcast.1, s32[1,32]{1,0:T(1,128)} %start_ref.1, bf16[4,4,512]{2,1,0:T(4,128)(2,1)} %q3_ref.1, bf16[4,1024]{1,0:T(4,128)(2,1)} %new_ref.1, bf16[512,512]{1,0:T(8,128)(2,1)} %basis_ref.1, bf16[2048,512]{1,0:T(8,128)(2,1)} %kv_hbm.1, bf16[2048,4096]{1,0:T(8,128)(2,1)} %w_hbm.1), custom_call_target="tpu_custom_call" | custom-call | tf_op jit(solution)/shard_map/pallas_call | solution.py:424
  39.0 1.3 %copy.9 = bf16[4,2048]{1,0:T(4,128)(2,1)} copy(bf16[4,2048]{1,0:T(4,128)(2,1)} %shard_map.73) | data formatting | bytes 32768

commit v4 on v3

--- a/solution.py
+++ b/solution.py
@@ -96,7 +96,7 @@
 
 def handoff_kernel(
     owner_ref, start_ref, q3_ref, new_ref, basis_ref, kv_hbm, w_hbm, out_ref,
-    kv, w, q_ref, qbuf, bbuf, gram_k, gram_v, qf, slotm_ref, mine, ssend, srecv, sdup, p_scr, tops,
+    kv, w, q_ref, qbuf, bbuf, proj, slotm_ref, mine, ssend, srecv, p_scr, tops,
     pblk, asend, arecv, tsend, trecv, x16, osend, orecv, outf,
     loc_sem, q1_sem, qs_sem, qr_sem, b_sem, s_sem, r_sem, as_sem, ar_sem, ts_sem, tr_sem, o_sem,
 ):
@@ -143,12 +143,20 @@
 
     q1 = remote(q_ref, qbuf.at[me, tp], q1_sem.at[0], q1_sem.at[1], me, oth)
     q1.start()
-    hb = bbuf.shape[2]
-    b1 = remote(
-        basis_ref.at[pl.ds(pl.multiple_of(dp * hb, hb), hb)], bbuf.at[tp, dp],
-        b_sem.at[0], b_sem.at[1], me, oth,
-    )
-    b1.start()
+    sib = 2 * lax.axis_index("ctx") + 1 - dp
+    hb = bbuf.shape[3]
+
+    def b_first(g):
+        return remote(
+            basis_ref.at[pl.ds(pl.multiple_of(g * HD + dp * hb, hb), hb)], bbuf.at[tp, g, dp],
+            b_sem.at[g], b_sem.at[4 + g], me, oth,
+        )
+
+    def b_second(g):
+        return remote(bbuf.at[oth, g, dp], bbuf.at[oth, g, dp], b_sem.at[8 + g], b_sem.at[12 + g], sib, tp)
+
+    for g in range(4):
+        b_first(g).start()
     qbuf[me, tp] = q_ref[...]
     q1.wait()
 
@@ -161,8 +169,10 @@
 
     lax.fori_loop(1, owners, q_start, 0)
 
-    bbuf[tp, 0] = basis_ref[:hb]
-    bbuf[tp, 1] = basis_ref[hb:]
+    for g in range(4):
+        for d in range(2):
+            r0 = g * HD + d * hb
+            bbuf[tp, g, d] = basis_ref[r0 : r0 + hb]
     req = owner_ref.shape[1]
     ri = lax.broadcasted_iota(i32, (req, req), 0)
     ci = lax.broadcasted_iota(i32, (req, req), 1)
@@ -193,15 +203,14 @@
         s = jnp.sum(qk[:, g * HD : (g + 1) * HD], axis=1, keepdims=True) * scale
         own = jnp.where(lane_g == g, s, own)
 
-    b1.wait()
-    sib = 2 * lax.axis_index("ctx") + 1 - dp
-    b2 = remote(bbuf.at[oth, dp], bbuf.at[oth, dp], b_sem.at[2], b_sem.at[3], sib, tp)
-    b2.start()
-    b2.wait()
-    full_k = bbuf[0].reshape(512, 512)
-    full_v = bbuf[1].reshape(512, 512)
-    gram_k[...] = dot(full_k, basis_ref[...], NT).astype(bf16)
-    gram_v[...] = dot(basis_ref[...], full_v, NT).astype(bf16)
+    kv_copy.wait()
+
+    def project(c, carry):
+        span = pl.ds(pl.multiple_of(c * cn, cn), cn)
+        proj[span, :] = dot(kv[span, :], basis_ref[...]).astype(bf16)
+        return carry
+
+    lax.fori_loop(0, CHUNKS, project, 0)
 
     def q_wait(i, c):
         o = lax.rem(me + i, owners)
@@ -212,22 +221,22 @@
 
     lax.fori_loop(1, owners, q_wait, 0)
     q_rows = qbuf[...].reshape(slots * 8, 512)
-    for g in range(4):
-        qf[g] = dot(q_rows[:, g * HD : (g + 1) * HD], gram_k[g * HD : (g + 1) * HD, :]).astype(bf16)
-    kv_copy.wait()
-
     low8 = lax.broadcasted_iota(i32, (8, cn), 0) < 4
-
-    def s_copy(c):
-        return remote(ssend.at[c], srecv.at[c], s_sem.at[c], r_sem.at[c], me, oth)
-
-    def score_chunk(c, carry):
-        span = pl.ds(pl.multiple_of(c * cn, cn), cn)
-        kvc = kv[span, :]
-        sm = slotm_ref[:, span]
-        parts = []
-        for g in range(4):
-            dense = dot(qf[g], kvc, NT)
+    half_rows = rows // 2
+
+    def s_copy(g):
+        return remote(ssend.at[g], srecv.at[g], s_sem.at[g], r_sem.at[g], me, oth)
+
+    def scores(g):
+        b_first(g).wait()
+        b_second(g).start()
+        b_second(g).wait()
+        qg = dot(q_rows[:, g * HD : (g + 1) * HD], bbuf[0, g].reshape(HD, 512)).astype(bf16)
+
+        def score_chunk(c, carry):
+            span = pl.ds(pl.multiple_of(c * cn, cn), cn)
+            sm = slotm_ref[:, span]
+            dense = dot(qg, proj[span, :], NT)
             folded = []
             for t in range(2):
                 acc = jnp.zeros((8, cn), f32)
@@ -235,44 +244,37 @@
                     for k2 in range(2):
                         r0 = o * 32 + t * 16 + k2 * 8
                         acc = jnp.where(sm == o * 4 + 2 * k2, dense[r0 : r0 + 8], acc)
-                folded.append(acc)
-            folded = [a + roll4(a) for a in folded]
-            parts.append(jnp.where(low8, folded[0], folded[1]))
-        parts = jnp.concatenate(parts, axis=0)
-        mine[c] = parts
-        ssend[c] = parts.astype(bf16)
-        s_copy(c).start()
-        return carry
-
-    lax.fori_loop(0, CHUNKS, score_chunk, 0)
-
-    def merge_chunk(c, carry):
-        span = pl.ds(pl.multiple_of(c * cn, cn), cn)
-        s_copy(c).wait()
-        both = (mine[c] + srecv[c].astype(f32)) * scale
-        for g in range(4):
-            part = both[g * 8 : (g + 1) * 8]
-            turned = roll4(part)
-            sdup[2 * g, :, span] = jnp.where(low8, part, turned)
-            sdup[2 * g + 1, :, span] = jnp.where(low8, turned, part)
-        return carry
-
-    lax.fori_loop(0, CHUNKS, merge_chunk, 0)
-
-    def soft(gt, carry):
-        s = sdup[gt]
+                folded.append(acc + roll4(acc))
+            mine[g, :, span] = jnp.where(low8, folded[0], folded[1])
+            return carry
+
+        lax.fori_loop(0, CHUNKS, score_chunk, 0)
+        ssend[g] = jnp.concatenate([mine[g, :, :half_rows], mine[g, :, half_rows:]], axis=0).astype(bf16)
+        s_copy(g).start()
+
+    def soften(g):
+        s_copy(g).wait()
+        got = srecv[g].astype(f32)
+        part = (mine[g] + jnp.concatenate([got[:8], got[8:]], axis=1)) * scale
+        turned = roll4(part)
+        low = lax.broadcasted_iota(i32, (8, rows), 0) < 4
         sm = slotm_ref[...]
-        top_tok = jnp.zeros((8, rows), f32)
-        for c in range(2 * owners):
-            live = sm == 2 * c
-            top = jnp.max(jnp.where(live, s, LOW), axis=1, keepdims=True)
-            tops[c, gt] = jnp.broadcast_to(top, (8, 128))
-            top_tok = jnp.where(live, top, top_tok)
-        top_tok = top_tok + roll4(top_tok)
-        p_scr[gt] = jnp.exp(s - top_tok)
-        return carry
-
-    lax.fori_loop(0, 8, soft, 0)
+        for t in range(2):
+            gt = 2 * g + t
+            s = jnp.where(low, part, turned) if t == 0 else jnp.where(low, turned, part)
+            top_tok = jnp.zeros((8, rows), f32)
+            for c in range(2 * owners):
+                live = sm == 2 * c
+                top = jnp.max(jnp.where(live, s, LOW), axis=1, keepdims=True)
+                tops[c, gt] = jnp.broadcast_to(top, (8, 128))
+                top_tok = jnp.where(live, top, top_tok)
+            p_scr[gt] = jnp.exp(s - top_tok - roll4(top_tok))
+
+    for g in range(4):
+        scores(g)
+        if g:
+            soften(g - 1)
+    soften(3)
 
     def a_copies(o, so):
         return [
@@ -294,11 +296,11 @@
                 tot.append(jnp.sum(both, axis=1, keepdims=True))
                 r0 = d * 128 + gt * 16
                 pblk[r0 : r0 + 16, :] = both.astype(bf16)
-        u = dot(pblk[...], kv[...]).astype(bf16)
+        u = dot(pblk[...], proj[...]).astype(bf16)
         stats = [jnp.full((16, 128), LOW, f32) for _ in range(2)]
         for g in range(4):
             rows_g = jnp.concatenate([u[d * 128 + g * 32 : d * 128 + (g + 1) * 32] for d in range(2)], axis=0)
-            a = dot(rows_g, gram_v[:, g * HD : (g + 1) * HD])
+            a = dot(rows_g, bbuf[1, g].reshape(HD, 512), NT)
             for d in range(2):
                 o = ctx * 2 + d
                 lse = []
@@ -416,7 +418,6 @@
     f32, bf16 = jnp.float32, jnp.bfloat16
     owners = lax.axis_size("ctx") * lax.axis_size("dp")
     rows = kv_rows.shape[0]
-    slots = owners * 4
     half_cols = out_weight.shape[1] // 2
     dma = pltpu.SemaphoreType.DMA
     vm = pl.BlockSpec(memory_space=pltpu.VMEM)
@@ -431,15 +432,12 @@
             pltpu.VMEM((2, out_weight.shape[0], half_cols), bf16),
             pltpu.VMEM((16, 512), bf16),
             pltpu.VMEM((owners, 2, 16, 512), bf16),
-            pltpu.VMEM((2, 2, 256, 512), bf16),
-            pltpu.VMEM((512, 512), bf16),
-            pltpu.VMEM((512, 512), bf16),
-            pltpu.VMEM((4, slots * 8, 512), bf16),
+            pltpu.VMEM((2, 4, 2, HD // 2, 512), bf16),
+            pltpu.VMEM((rows, 512), bf16),
             pltpu.VMEM((8, rows), jnp.int32),
-            pltpu.VMEM((CHUNKS, 32, rows // CHUNKS), f32),
-            pltpu.VMEM((CHUNKS, 32, rows // CHUNKS), bf16),
-            pltpu.VMEM((CHUNKS, 32, rows // CHUNKS), bf16),
-            pltpu.VMEM((8, 8, rows), f32),
+            pltpu.VMEM((4, 8, rows), f32),
+            pltpu.VMEM((4, 16, rows // 2), bf16),
+            pltpu.VMEM((4, 16, rows // 2), bf16),
             pltpu.VMEM((8, 8, rows), f32),
             pltpu.VMEM((2 * owners, 8, 8, 128), f32),
             pltpu.VMEM((256, rows), bf16),
@@ -451,8 +449,8 @@
             pltpu.VMEM((8, half_cols // 2), f32),
             pltpu.VMEM((8, half_cols // 2), f32),
             pltpu.VMEM((8, half_cols // 2), f32),
-            dma((3,)), dma((2,)), dma((owners,)), dma((owners,)), dma((4,)),
-            dma((CHUNKS,)), dma((CHUNKS,)),
+            dma((3,)), dma((2,)), dma((owners,)), dma((owners,)), dma((16,)),
+            dma((4,)), dma((4,)),
             dma((2 * owners,)), dma((2 * owners,)), dma((owners,)), dma((owners,)), dma((2,)),
         ],
         compiler_params=pltpu.CompilerParams(

time: 40.6 us -> 45.5 us (1.12)
  Pallas kernels: 39 us -> 44 us
    pallas_call x1, Pallas kernels: 39 us -> 44 us  [fused(): pl.pallas_call(handoff_kernel, out_shape=jax.ShapeDtypeStruct((4, half_co...]
where the time goes in v4:
time: 45.5 us; the launch traced here: 45.3 us
  Pallas kernels  44 us (97%)
  local copies, waits for them, and re-layouts  1.33 us (3%)
    pallas_call x1, Pallas kernels, fused(): pl.pallas_call(handoff_kernel, out_shape=jax.ShapeDtypeStruct((4, half_co...  44 us
    unnamed x1, local copies, waits for them, and re-layouts  1.33 us

profile of v4, /device:TPU:0, one launch (start us, length us, event | category | flops | bytes accessed | tf_op | source)
XLA Modules:
  0.0 45.3 jit_solution(4513900877080477268)
XLA Ops:
  0.0 44.0 %shard_map.73 = bf16[4,2048]{1,0:T(4,128)(2,1)} custom-call(s32[1,32]{1,0:T(1,128)} %bitcast.1, s32[1,32]{1,0:T(1,128)} %start_ref.1, bf16[4,4,512]{2,1,0:T(4,128)(2,1)} %q3_ref.1, bf16[4,1024]{1,0:T(4,128)(2,1)} %new_ref.1, bf16[512,512]{1,0:T(8,128)(2,1)} %basis_ref.1, bf16[2048,512]{1,0:T(8,128)(2,1)} %kv_hbm.1, bf16[2048,4096]{1,0:T(8,128)(2,1)} %w_hbm.1), custom_call_target="tpu_custom_call" | custom-call | tf_op jit(solution)/shard_map/pallas_call | solution.py:425
  44.0 1.3 %copy.9 = bf16[4,2048]{1,0:T(4,128)(2,1)} copy(bf16[4,2048]{1,0:T(4,128)(2,1)} %shard_map.73) | data formatting | bytes 32768

commit v5 on v4

--- a/solution.py
+++ b/solution.py
@@ -155,7 +155,7 @@
     def b_second(g):
         return remote(bbuf.at[oth, g, dp], bbuf.at[oth, g, dp], b_sem.at[8 + g], b_sem.at[12 + g], sib, tp)
 
-    for g in range(4):
+    for g in range(2):
         b_first(g).start()
     qbuf[me, tp] = q_ref[...]
     q1.wait()
@@ -212,6 +212,15 @@
 
     lax.fori_loop(0, CHUNKS, project, 0)
 
+    def pass_on(g):
+        b_first(g).wait()
+        b_second(g).start()
+        if g < 2:
+            b_first(g + 2).start()
+
+    pass_on(0)
+    pass_on(1)
+
     def q_wait(i, c):
         o = lax.rem(me + i, owners)
         cp = q_copy(o, o)
@@ -228,8 +237,6 @@
         return remote(ssend.at[g], srecv.at[g], s_sem.at[g], r_sem.at[g], me, oth)
 
     def scores(g):
-        b_first(g).wait()
-        b_second(g).start()
         b_second(g).wait()
         qg = dot(q_rows[:, g * HD : (g + 1) * HD], bbuf[0, g].reshape(HD, 512)).astype(bf16)
 
@@ -270,10 +277,15 @@
                 top_tok = jnp.where(live, top, top_tok)
             p_scr[gt] = jnp.exp(s - top_tok - roll4(top_tok))
 
-    for g in range(4):
-        scores(g)
-        if g:
-            soften(g - 1)
+    scores(0)
+    pass_on(2)
+    scores(1)
+    pass_on(3)
+    soften(0)
+    scores(2)
+    soften(1)
+    scores(3)
+    soften(2)
     soften(3)
 
     def a_copies(o, so):

time: 45.5 us -> 42.2 us (0.927)
  Pallas kernels: 44 us -> 40.6 us
    pallas_call x1, Pallas kernels: 44 us -> 40.6 us  [fused(): pl.pallas_call(handoff_kernel, out_shape=jax.ShapeDtypeStruct((4, half_co...]
where the time goes in v5:
time: 42.2 us; the launch traced here: 41.9 us
  Pallas kernels  40.6 us (96%)
  local copies, waits for them, and re-layouts  1.33 us (3%)
    pallas_call x1, Pallas kernels, fused(): pl.pallas_call(handoff_kernel, out_shape=jax.ShapeDtypeStruct((4, half_co...  40.6 us
    unnamed x1, local copies, waits for them, and re-layouts  1.33 us

profile of v5, /device:TPU:0, one launch (start us, length us, event | category | flops | bytes accessed | tf_op | source)
XLA Modules:
  0.0 41.9 jit_solution(14835179322180434057)
XLA Ops:
  0.0 40.6 %shard_map.73 = bf16[4,2048]{1,0:T(4,128)(2,1)} custom-call(s32[1,32]{1,0:T(1,128)} %bitcast.1, s32[1,32]{1,0:T(1,128)} %start_ref.1, bf16[4,4,512]{2,1,0:T(4,128)(2,1)} %q3_ref.1, bf16[4,1024]{1,0:T(4,128)(2,1)} %new_ref.1, bf16[512,512]{1,0:T(8,128)(2,1)} %basis_ref.1, bf16[2048,512]{1,0:T(8,128)(2,1)} %kv_hbm.1, bf16[2048,4096]{1,0:T(8,128)(2,1)} %w_hbm.1), custom_call_target="tpu_custom_call" | custom-call | tf_op jit(solution)/shard_map/pallas_call | solution.py:437
  40.6 1.3 %copy.9 = bf16[4,2048]{1,0:T(4,128)(2,1)} copy(bf16[4,2048]{1,0:T(4,128)(2,1)} %shard_map.73) | data formatting | bytes 32768
